TPU v7x, 32 devices: a whole 2x2x4 slice. The times are simulated.
32 devices in a mesh: area: 4 (over z), dev: 8 (over y, x, core).
Axes of the slice: x: 2, y: 2, z: 4, core: 2. Of those that a mesh axis runs over, the one named last changes fastest.
Arguments:
- wave_fwd: float32 [3, 16384, 128], P(None, ('area', 'dev')), may hold values from -6 to 6
- wave_bwd: float32 [3, 16384, 128], P(None, ('area', 'dev')), may hold values from -6 to 6
- seg_reflect: float32 [3, 16384], P(None, ('area', 'dev')), may hold values from 0.04 to 0.4
- seg_count: int32 [32, 64], P(('area', 'dev')), may hold values from 1 to 24, 512 in all within a row
- modal_admit: float32 [3, 2048], P(None, ('area', 'dev')), may hold values from 0.02 to 0.2
- modal_transform: float32 [3, 3], replicated, may hold values from -3.5 to 3.5
- end_slot: int32 [2048, 2], P(('area', 'dev')), may hold values from 0 to 255, as said below
- recv_bus: int32 [32, 256], P(('area', 'dev')), may hold values from -1 to 63, as said below
- bus_impedance: float32 [3, 3, 2048], P(None, None, ('area', 'dev')), as said below
- link_bus: int32 [192, 2], P('area'), may hold values from 0 to 511, as said below
- link_resist: float32 [192], P('area'), may hold values from 0.5 to 5
- source_current: float32 [4, 2048, 3, 128], P(None, ('area', 'dev')), may hold values from -6 to 6
Outputs:
- bus_voltage: float32 [4, 2048, 3, 128], P(None, ('area', 'dev'))
- final_fwd: float32 [3, 16384, 128], P(None, ('area', 'dev'))
- final_bwd: float32 [3, 16384, 128], P(None, ('area', 'dev'))
Inputs may be any that keep to these rules, and one draw needn't show every extreme that they name: `end_slot`: entry [l, s] is the slot of end s (0 sending, 1 receiving) of line l within its device's 32 blocks of 8 slots, block q // 8 going to owner device q // 8. The slots of one device are distinct. Every device fills all 8 slots of the block for some owner, and one owner receives 8 ends from every device. `recv_bus`: row r, column s * 8 + c: the local bus of device r to which slot c of device s's block for r attaches, and -1 exactly where no end of device s holds that slot. `link_bus`: the two buses of a link differ. `bus_impedance`: each bus's 3x3 matrix is symmetric with a positive diagonal larger than the sum of its row's other magnitudes.
All inputs are finite; a program needn't handle non-finite values.
Results may differ from a plain program's by a relative error of at most 0.00012.
Values sent between devices are 32-bit elements; how exact they have to be, the bound alone decides.
A program may use at most 64 MiB of HBM per device.

v0:
```python
import jax
import jax.numpy as jnp
from jax import lax
from jax.sharding import PartitionSpec as P

STEPS = 4


def solve_links(factor, rhs):
    lower = lax.linalg.triangular_solve(factor, rhs, left_side=True, lower=True)
    return lax.linalg.triangular_solve(factor, lower, left_side=True, lower=True, transpose_a=True)


def send_ends(rows):
    return lax.all_to_all(rows, ("area", "dev"), split_axis=0, concat_axis=0, tiled=True)


def return_volts(rows):
    return lax.all_to_all(rows, ("area", "dev"), split_axis=0, concat_axis=0, tiled=True)


def on_device(
    wave_fwd,
    wave_bwd,
    seg_reflect,
    seg_count,
    modal_admit,
    modal_transform,
    end_slot,
    recv_bus,
    bus_impedance,
    link_bus,
    link_resist,
    source_current,
):
    exact = lax.Precision.HIGHEST
    cases = wave_fwd.shape[2]
    line_total = end_slot.shape[0]
    counts = seg_count[0]
    first = jnp.cumsum(counts) - counts
    last = first + counts - 1
    bus_total = bus_impedance.shape[2]
    link_total = link_bus.shape[0]
    bus_index = jnp.arange(bus_total, dtype=jnp.int32) + lax.axis_index("dev") * bus_total
    incidence = (bus_index[:, None] == link_bus[None, :, 0]).astype(jnp.float32) - (
        bus_index[:, None] == link_bus[None, :, 1]
    ).astype(jnp.float32)
    partial_value = jnp.einsum(
        "bl,ijb,bm->limj", incidence, bus_impedance, incidence, precision=exact
    ).reshape(3 * link_total, 3 * link_total)
    matrix = lax.psum(partial_value, "dev") + jnp.diag(jnp.repeat(link_resist, 3))
    factor = jnp.linalg.cholesky(matrix)
    place_overall_sum = recv_bus.shape[1]
    one_hot = (jnp.arange(bus_total, dtype=jnp.int32)[:, None] == recv_bus).astype(jnp.float32)
    flat_slot = end_slot.reshape(-1)
    reflect_next = jnp.roll(seg_reflect, -1, axis=1)
    forward, backward = (wave_fwd, wave_bwd)
    voltages = []
    for step in range(STEPS):
        arriving = jnp.stack([backward[:, first, :], forward[:, last, :]], axis=2)
        history = 2.0 * jnp.einsum(
            "mi,mlsk->lsik",
            modal_transform,
            modal_admit[:, :, None, None] * arriving,
            precision=exact,
        )
        send_rows = (
            jnp.zeros((place_overall_sum, 3 * cases), jnp.float32)
            .at[flat_slot]
            .set(history.reshape(2 * line_total, 3 * cases))
        )
        received = send_ends(send_rows)
        summed = jnp.dot(
            one_hot, received, precision=exact, preferred_element_type=jnp.float32
        ).reshape(bus_total, 3, cases)
        inject = source_current[step] + summed
        open_volts = jnp.einsum("ijb,bjk->bik", bus_impedance, inject, precision=exact)
        sources = jnp.einsum("bl,bik->lik", incidence, open_volts, precision=exact).reshape(
            3 * link_total, cases
        )
        owned = lax.psum_scatter(sources, "dev", scatter_dimension=1, tiled=True)
        current = lax.all_gather(solve_links(factor, owned), "dev", axis=1, tiled=True)
        current = current.reshape(link_total, 3, cases)
        net = inject - jnp.einsum("bl,lik->bik", incidence, current, precision=exact)
        volts = jnp.einsum("ijb,bjk->bik", bus_impedance, net, precision=exact)
        voltages.append(volts)
        slot_volts = jnp.dot(
            one_hot.T,
            volts.reshape(bus_total, 3 * cases),
            precision=exact,
            preferred_element_type=jnp.float32,
        )
        back_rows = return_volts(slot_volts)
        end_volts = back_rows[flat_slot].reshape(line_total, 2, 3, cases)
        outgoing = (
            jnp.einsum("mi,lsik->mlsk", modal_transform, end_volts, precision=exact) - arriving
        )
        fwd_next = (1.0 - seg_reflect)[:, :, None] * jnp.roll(forward, 1, axis=1) + seg_reflect[
            :, :, None
        ] * backward
        fwd_next = fwd_next.at[:, first, :].set(outgoing[:, :, 0, :])
        bwd_next = (1.0 - reflect_next)[:, :, None] * jnp.roll(backward, -1, axis=1) + reflect_next[
            :, :, None
        ] * forward
        bwd_next = bwd_next.at[:, last, :].set(outgoing[:, :, 1, :])
        forward, backward = (fwd_next, bwd_next)
    return (jnp.stack(voltages), forward, backward)


def solution(mesh):
    in_specs = (
        P(None, ("area", "dev"), None),
        P(None, ("area", "dev"), None),
        P(None, ("area", "dev")),
        P(("area", "dev"), None),
        P(None, ("area", "dev")),
        P(),
        P(("area", "dev"), None),
        P(("area", "dev"), None),
        P(None, None, ("area", "dev")),
        P("area", None),
        P("area"),
        P(None, ("area", "dev"), None, None),
    )
    out_specs = (
        P(None, ("area", "dev"), None, None),
        P(None, ("area", "dev"), None),
        P(None, ("area", "dev"), None),
    )
    return jax.shard_map(
        on_device, mesh=mesh, in_specs=in_specs, out_specs=out_specs, check_vma=False
    )
```

profile of v0, /device:TPU:0, one launch (start us, length us, event | category | flops | bytes accessed | tf_op | source)
XLA Modules:
  0.0 491.2 jit_solution(10305870664416190752)
XLA Ops:
  16.4 7.4 %all-to-all-start = ((f32[32,8,384]{2,1,0:T(8,128)}), f32[32,8,384]{2,1,0:T(8,128)}, u32[]{:S(2)}, u32[]{:S(2)}) async-start(f32[32,8,384]{2,1,0:T(8,128)} %bitcast.11), calls=%async_computation | async-start | bytes 786432 | tf_op jit(solution)/shard_map/all_to_all | solution.py:15
  31.9 51.1 %all-reduce.7.cloned.1.call-done = f32[144,144]{1,0:T(8,128)} async-done(((f32[144,144]{1,0:T(8,128)}), f32[144,144]{1,0:T(8,128)}) %all-reduce.7.cloned.1.call-update) | async-done | bytes 82960 | tf_op jit(solution)/shard_map/psum | solution.py:51
  85.2 11.7 %cholesky.50 = f32[128,128]{1,0:T(8,128)S(1)} custom-call(f32[128,128]{1,0:T(8,128)S(1)} %cholesky.121), custom_call_target="Cholesky" | custom-call | tf_op jit(solution)/shard_map/jit(cholesky)/cholesky | solution.py:52
  97.0 9.8 %custom-call.17 = f32[1,128,128]{1,2,0:T(8,128)S(1)} custom-call(f32[1,128,128]{2,1,0:T(8,128)S(1)} %get-tuple-element.103), custom_call_target="InvertDiagBlocksLowerTriangular" | custom-call | tf_op jit(solution)/shard_map/jit(cholesky)/cholesky | solution.py:52
  115.5 19.7 %custom-call.25 = f32[2,128,128]{1,2,0:T(8,128)S(1)} custom-call(f32[2,128,128]{2,1,0:T(8,128)S(1)} %pad_maximum_fusion.9), custom_call_target="InvertDiagBlocksLowerTriangular" | custom-call | tf_op jit(solution)/shard_map/triangular_solve/custom-call.4 | solution.py:11
  135.2 14.8 %reduce-scatter.13.cloned.1.call-done = f32[16,144]{1,0:T(8,128)} async-done(((f32[128,144]{1,0:T(8,128)}), f32[16,144]{1,0:T(8,128)}) %reduce-scatter.13.cloned.1.call-update) | async-done | bytes 9232
  152.5 9.4 %all_gather.12 = f32[144,128]{0,1:T(8,128)S(1)} all-gather(f32[144,16]{0,1:T(8,128)S(1)} %pad_maximum_fusion.10), channel_id=1, replica_groups=mesh['area'=4,'dev'=8] {'dev'}, dimensions={1}, use_global_device_ids=true | all-gather | bytes 82944 | tf_op jit(solution)/shard_map/all_gather | solution.py:82
  164.2 4.6 all-to-all-start.1
  172.7 5.0 %fusion.5 = f32[3,512,128]{2,0,1:T(4,128)S(1)} fusion(f32[3,511,128]{2,0,1:T(4,128)} %copy.234, f32[3,1,128]{2,0,1:T(4,128)S(1)} %copy.235, f32[3,512]{0,1:T(8,128)S(1)} %copy.117, f32[3,512]{0,1:T(8,128)S(1)} %copy.114, f32[3,512,128]{2,1,0:T(8,128)S(1)} %copy-done.1), kind=kLoop, calls=%fused_computation.61 | loop fusion | flops 786432 | bytes 2371584 | tf_op jit(solution)/shard_map/add | solution.py:98
  177.7 4.5 fusion.4
  194.3 18.9 %all_to_all.84 = f32[32,8,384]{2,1,0:T(8,128)} all-to-all(f32[32,8,384]{2,1,0:T(8,128)S(1)} %bitcast.344), channel_id=1, replica_groups=mesh['area'=4,'dev'=8] {'area','dev'}, dimensions={0} | all-to-all | bytes 786432 | tf_op jit(solution)/shard_map/all_to_all | solution.py:15
  218.0 31.6 %reduce-scatter.15.cloned.1.call-done = f32[16,144]{1,0:T(8,128)} async-done(((f32[128,144]{1,0:T(8,128)}), f32[16,144]{1,0:T(8,128)}) %reduce-scatter.15.cloned.1.call-update) | async-done | bytes 9232
  253.5 9.6 %all_gather.13 = f32[144,128]{0,1:T(8,128)S(1)} all-gather(f32[144,16]{0,1:T(8,128)S(1)} %pad_maximum_fusion.11), channel_id=1, replica_groups=mesh['area'=4,'dev'=8] {'dev'}, dimensions={1}, use_global_device_ids=true | all-gather | bytes 82944 | tf_op jit(solution)/shard_map/all_gather | solution.py:82
  266.0 4.7 all-to-all-start.3
  276.8 7.1 %all-to-all-done.3 = f32[32,8,384]{2,1,0:T(8,128)} async-done(((f32[32,8,384]{2,1,0:T(8,128)}), f32[32,8,384]{2,1,0:T(8,128)}, u32[]{:S(2)}, u32[]{:S(2)}) %all-to-all-start.3) | async-done | bytes 393248 | tf_op jit(solution)/shard_map/all_to_all | solution.py:19
  296.0 15.6 %all_to_all.85 = f32[32,8,384]{2,1,0:T(8,128)S(1)} all-to-all(f32[32,8,384]{2,1,0:T(8,128)S(1)} %bitcast.347), channel_id=1, replica_groups=mesh['area'=4,'dev'=8] {'area','dev'}, dimensions={0} | all-to-all | bytes 786432 | tf_op jit(solution)/shard_map/all_to_all | solution.py:15
  314.8 31.5 %reduce-scatter.17.cloned.1.call-done = f32[16,144]{1,0:T(8,128)} async-done(((f32[128,144]{1,0:T(8,128)}), f32[16,144]{1,0:T(8,128)}) %reduce-scatter.17.cloned.1.call-update) | async-done | bytes 9232
  350.2 9.2 %all_gather.14 = f32[144,128]{0,1:T(8,128)S(1)} all-gather(f32[144,16]{0,1:T(8,128)S(1)} %pad_maximum_fusion.12), channel_id=1, replica_groups=mesh['area'=4,'dev'=8] {'dev'}, dimensions={1}, use_global_device_ids=true | all-gather | bytes 82944 | tf_op jit(solution)/shard_map/all_gather | solution.py:82
  361.7 4.7 all-to-all-start.5
  372.7 6.9 %all-to-all-done.5 = f32[32,8,384]{2,1,0:T(8,128)} async-done(((f32[32,8,384]{2,1,0:T(8,128)}), f32[32,8,384]{2,1,0:T(8,128)}, u32[]{:S(2)}, u32[]{:S(2)}) %all-to-all-start.5) | async-done | bytes 393248 | tf_op jit(solution)/shard_map/all_to_all | solution.py:19
  391.7 15.6 %all_to_all.86 = f32[32,8,384]{2,1,0:T(8,128)S(1)} all-to-all(f32[32,8,384]{2,1,0:T(8,128)S(1)} %bitcast.342), channel_id=1, replica_groups=mesh['area'=4,'dev'=8] {'area','dev'}, dimensions={0} | all-to-all | bytes 786432 | tf_op jit(solution)/shard_map/all_to_all | solution.py:15
  414.0 28.0 %reduce-scatter.19.cloned.1.call-done = f32[16,144]{1,0:T(8,128)} async-done(((f32[128,144]{1,0:T(8,128)}), f32[16,144]{1,0:T(8,128)}) %reduce-scatter.19.cloned.1.call-update) | async-done | bytes 9232
  445.9 9.2 %all_gather.15 = f32[144,128]{0,1:T(8,128)S(1)} all-gather(f32[144,16]{0,1:T(8,128)S(1)} %pad_maximum_fusion.13), channel_id=1, replica_groups=mesh['area'=4,'dev'=8] {'dev'}, dimensions={1}, use_global_device_ids=true | all-gather | bytes 82944 | tf_op jit(solution)/shard_map/all_gather | solution.py:82
  458.1 4.8 all-to-all-start.7
  (357 shorter events, 138.5 us)
Async XLA Ops:
  16.4 94.9 %all-to-all-start = ((f32[32,8,384]{2,1,0:T(8,128)}), f32[32,8,384]{2,1,0:T(8,128)}, u32[]{:S(2)}, u32[]{:S(2)}) async-start(f32[32,8,384]{2,1,0:T(8,128)} %bitcast.11), calls=%async_computation | async-start | bytes 786432 | tf_op jit(solution)/shard_map/all_to_all | solution.py:15
  23.8 59.2 %all-reduce.7.cloned.1.call-start = ((), (), s32[]{:S(2)}) async-start(), calls=%async_computation.12 | async-start | bytes 294912 | tf_op jit(solution)/shard_map/psum | solution.py:51
  29.8 82.7 %copy-start.40 = (s32[1,256]{1,0:T(1,128)S(1)}, s32[1,256]{1,0:T(1,128)}, u32[]{:S(2)}) copy-start(s32[1,256]{1,0:T(1,128)} %param.23) | copy-start | bytes 3076
  29.8 84.6 %copy-start.43 = (s32[48]{0:T(128)S(1)}, s32[48]{0:T(128)}, u32[]{:S(2)}) copy-start(s32[48]{0:T(128)} %copy-done.42) | copy-start | bytes 580
  29.8 84.6 %copy-start.46 = (s32[48]{0:T(128)S(1)}, s32[48]{0:T(128)}, u32[]{:S(2)}) copy-start(s32[48]{0:T(128)} %copy-done.45) | copy-start | bytes 580
  29.8 84.6 %copy-start.49 = (s32[64]{0:T(128)S(1)}, s32[64]{0:T(128)}, u32[]{:S(2)}) copy-start(s32[64]{0:T(128)} %copy-done.48) | copy-start | bytes 772
  29.8 120.2 %reduce-scatter.13.cloned.1.call-start = ((), (), s32[]{:S(2)}) async-start(), calls=%async_computation.13 | async-start | bytes 147456
  85.2 83.6 %copy-start.69 = (s32[128]{0:T(128)S(1)}, s32[128]{0:T(128)}, u32[]{:S(2)}) copy-start(s32[128]{0:T(128)} %copy-done.68) | copy-start | bytes 1540
  96.9 71.9 %copy-start.2 = (f32[3,512,128]{2,1,0:T(8,128)S(1)}, f32[3,512,128]{2,1,0:T(8,128)}, u32[]{:S(2)}) copy-start(f32[3,512,128]{2,1,0:T(8,128)} %param.16) | copy-start | bytes 2359300
  97.0 72.1 %copy-start.1 = (f32[3,512,128]{2,1,0:T(8,128)S(1)}, f32[3,512,128]{2,1,0:T(8,128)}, u32[]{:S(2)}) copy-start(f32[3,512,128]{2,1,0:T(8,128)} %param.17) | copy-start | bytes 2359300
  111.2 53.0 %copy-start.28 = (f32[144,144]{1,0:T(8,128)}, f32[144,144]{1,0:T(8,128)S(1)}, u32[]{:S(2)}) copy-start(f32[144,144]{1,0:T(8,128)S(1)} %select_select_fusion) | copy-start | bytes 248836
  164.2 18.1 %all-to-all-start.1 = ((f32[32,8,384]{2,1,0:T(8,128)}), f32[32,8,384]{2,1,0:T(8,128)S(1)}, u32[]{:S(2)}, u32[]{:S(2)}) async-start(f32[32,8,384]{2,1,0:T(8,128)} %fusion.58), calls=%async_computation.1 | async-start | bytes 786432 | tf_op jit(solution)/shard_map/all_to_all | solution.py:19
  168.8 80.8 %reduce-scatter.15.cloned.1.call-start = ((), (), s32[]{:S(2)}) async-start(), calls=%async_computation.14 | async-start | bytes 147456
  172.7 98.3 %copy-start.9 = (f32[3,512]{0,1:T(8,128)}, f32[3,512]{0,1:T(8,128)S(1)}, u32[]{:S(2)}) copy-start(f32[3,512]{0,1:T(8,128)S(1)} %copy.109) | copy-start | bytes 18436
  183.2 67.1 %copy-start.16 = (f32[2,128,128]{1,2,0:T(8,128)S(1)}, f32[2,128,128]{1,2,0:T(8,128)}, u32[]{:S(2)}) copy-start(f32[2,128,128]{1,2,0:T(8,128)} %copy-done.15) | copy-start | bytes 393220
  266.0 17.9 %all-to-all-start.3 = ((f32[32,8,384]{2,1,0:T(8,128)}), f32[32,8,384]{2,1,0:T(8,128)}, u32[]{:S(2)}, u32[]{:S(2)}) async-start(f32[32,8,384]{2,1,0:T(8,128)} %fusion.56), calls=%async_computation.3 | async-start | bytes 786432 | tf_op jit(solution)/shard_map/all_to_all | solution.py:19
  270.7 75.6 %reduce-scatter.17.cloned.1.call-start = ((), (), s32[]{:S(2)}) async-start(), calls=%async_computation.15 | async-start | bytes 147456
  286.0 61.1 %copy-start.17 = (f32[2,128,128]{1,2,0:T(8,128)S(1)}, f32[2,128,128]{1,2,0:T(8,128)}, u32[]{:S(2)}) copy-start(f32[2,128,128]{1,2,0:T(8,128)} %copy-done.15) | copy-start | bytes 393220
  361.7 17.9 %all-to-all-start.5 = ((f32[32,8,384]{2,1,0:T(8,128)}), f32[32,8,384]{2,1,0:T(8,128)}, u32[]{:S(2)}, u32[]{:S(2)}) async-start(f32[32,8,384]{2,1,0:T(8,128)} %fusion.54), calls=%async_computation.5 | async-start | bytes 786432 | tf_op jit(solution)/shard_map/all_to_all | solution.py:19
  366.4 75.6 %reduce-scatter.19.cloned.1.call-start = ((), (), s32[]{:S(2)}) async-start(), calls=%async_computation.16 | async-start | bytes 147456
  410.5 44.7 %copy-start.27 = (f32[64,3,128]{2,0,1:T(8,128)S(1)}, f32[64,3,128]{2,0,1:T(8,128)}, u32[]{:S(2)}) copy-start(f32[64,3,128]{2,0,1:T(8,128)} %copy-done.26) | copy-start | bytes 294916
  410.5 52.4 %copy-start.4 = (f32[3,512]{0,1:T(8,128)S(1)}, f32[3,512]{0,1:T(8,128)}, u32[]{:S(2)}) copy-start(f32[3,512]{0,1:T(8,128)} %copy-done.3) | copy-start | bytes 18436
  414.0 52.9 %copy-start.8 = (f32[3,512]{0,1:T(8,128)S(1)}, f32[3,512]{0,1:T(8,128)}, u32[]{:S(2)}) copy-start(f32[3,512]{0,1:T(8,128)} %copy-done.5) | copy-start | bytes 18436
  458.1 18.0 %all-to-all-start.7 = ((f32[32,8,384]{2,1,0:T(8,128)}), f32[32,8,384]{2,1,0:T(8,128)S(1)}, u32[]{:S(2)}, u32[]{:S(2)}) async-start(f32[32,8,384]{2,1,0:T(8,128)} %fusion.52), calls=%async_computation.7 | async-start | bytes 786432 | tf_op jit(solution)/shard_map/all_to_all | solution.py:19
  (57 other events, 576.7 us)
Sparse Core Ops, SparseCore 0:
  29.9 53.0 all-reduce.6
  115.6 34.3 reduce-scatter.12
  218.2 31.3 reduce-scatter.14
  314.9 31.3 reduce-scatter.16
  410.6 31.3 reduce-scatter.18
where the time goes:
time: 497 us; the launch traced here: 491 us
  waiting for transfers between devices  175 us (35%)
  blocking collectives  87.5 us (18%)
  other arithmetic  76.1 us (15%)
  local copies, waits for them, and re-layouts  69.5 us (14%)
  matrix products  39.5 us (8%)
  starting transfers between devices  26.8 us (5%)
  between operations  17.3 us (3%)
    unnamed x9, waiting for transfers between devices  106 us
    psum x1, waiting for transfers between devices, on_device(): lax.psum(partial_value, 'dev') + jnp.diag(jnp.repeat(link_resist, 3))  51.1 us
    all_to_all x3, blocking collectives, send_ends(): lax.all_to_all(rows, ('area', 'dev'), split_axis=0, concat_axis=0, tiled=...  50.2 us
    all_gather x4, blocking collectives, on_device(): lax.all_gather(solve_links(factor, owned), 'dev', axis=1, tiled=True)  37.3 us
    another operation x7, other arithmetic, on_device(): factor = jnp.linalg.cholesky(matrix)  24.3 us
    another operation x10, other arithmetic, solve_links(): lax.linalg.triangular_solve(factor, lower, left_side=True, lower=True, tr...  20 us
    all_to_all x4, starting transfers between devices, return_volts(): lax.all_to_all(rows, ('area', 'dev'), split_axis=0, concat_axis=0, tiled=...  18.8 us
    all_to_all x4, waiting for transfers between devices, return_volts(): lax.all_to_all(rows, ('area', 'dev'), split_axis=0, concat_axis=0, tiled=...  17.5 us
  transfers between devices with their start and end apart: 10, of which 8 were waited for; matrix products, arithmetic and copies ran while one was open for 19% of the time, Pallas kernels for 0%

commit v1 on v0

--- a/solution.py
+++ b/solution.py
@@ -4,6 +4,12 @@
 from jax.sharding import PartitionSpec as P
 
 STEPS = 4
+
+
+def add_all(value, axis):
+    blocks = lax.all_gather(value, axis, axis=0, tiled=False)
+    summed = blocks.sum(axis=0)
+    return summed
 
 
 def solve_links(factor, rhs):
@@ -48,7 +54,7 @@
     partial_value = jnp.einsum(
         "bl,ijb,bm->limj", incidence, bus_impedance, incidence, precision=exact
     ).reshape(3 * link_total, 3 * link_total)
-    matrix = lax.psum(partial_value, "dev") + jnp.diag(jnp.repeat(link_resist, 3))
+    matrix = add_all(partial_value, "dev") + jnp.diag(jnp.repeat(link_resist, 3))
     factor = jnp.linalg.cholesky(matrix)
     place_overall_sum = recv_bus.shape[1]
     one_hot = (jnp.arange(bus_total, dtype=jnp.int32)[:, None] == recv_bus).astype(jnp.float32)

time: 497 us -> 476 us (0.958)
  waiting for transfers between devices: 175 us -> 142 us
  blocking collectives: 87.5 us -> 101 us
    psum x1 -> x0, waiting for transfers between devices: 51.1 us -> none  [on_device(): lax.psum(partial_value, 'dev') + jnp.diag(jnp.repeat(link_resist, 3))]
    unnamed x9 -> x8, waiting for transfers between devices: 106 us -> 124 us
    all_gather x0 -> x1, blocking collectives: none -> 13.2 us  [add_all(): blocks = lax.all_gather(value, axis, axis=0, tiled=False)]
    unnamed x159 -> x157, local copies, waits for them, and re-layouts: 12.9 us -> 12.8 us
  transfers between devices with their start and end apart: 10 -> 9, of which waited for: 8 -> 7; matrix products, arithmetic and copies ran while one was open for 19% -> 19% of each run, Pallas kernels for 0% -> 0%
where the time goes in v1:
time: 476 us; the launch traced here: 470 us
  waiting for transfers between devices  142 us (30%)
  blocking collectives  101 us (21%)
  other arithmetic  74.9 us (16%)
  local copies, waits for them, and re-layouts  69.6 us (15%)
  matrix products  39.2 us (8%)
  starting transfers between devices  26.6 us (6%)
  between operations  17.2 us (4%)
    unnamed x8, waiting for transfers between devices  124 us
    all_to_all x3, blocking collectives, send_ends(): lax.all_to_all(rows, ('area', 'dev'), split_axis=0, concat_axis=0, tiled=...  50.2 us
    all_gather x4, blocking collectives, on_device(): lax.all_gather(solve_links(factor, owned), 'dev', axis=1, tiled=True)  37.3 us
    another operation x7, other arithmetic, on_device(): factor = jnp.linalg.cholesky(matrix)  24.4 us
    another operation x10, other arithmetic, solve_links(): lax.linalg.triangular_solve(factor, lower, left_side=True, lower=True, tr...  20 us
    all_to_all x4, starting transfers between devices, return_volts(): lax.all_to_all(rows, ('area', 'dev'), split_axis=0, concat_axis=0, tiled=...  18.8 us
    all_to_all x4, waiting for transfers between devices, return_volts(): lax.all_to_all(rows, ('area', 'dev'), split_axis=0, concat_axis=0, tiled=...  17.4 us
    add x4, other arithmetic, on_device(): (1.0 - seg_reflect)[:, :, None] * jnp.roll(forward, 1, axis=1)  15.5 us
  transfers between devices with their start and end apart: 9, of which 7 were waited for; matrix products, arithmetic and copies ran while one was open for 19% of the time, Pallas kernels for 0%

profile of v1, /device:TPU:0, one launch (start us, length us, event | category | flops | bytes accessed | tf_op | source)
XLA Modules:
  0.0 469.9 jit_solution(14852886155102805950)
XLA Ops:
  16.4 7.4 %all-to-all-start = ((f32[32,8,384]{2,1,0:T(8,128)}), f32[32,8,384]{2,1,0:T(8,128)}, u32[]{:S(2)}, u32[]{:S(2)}) async-start(f32[32,8,384]{2,1,0:T(8,128)} %bitcast.11), calls=%async_computation | async-start | bytes 786432 | tf_op jit(solution)/shard_map/all_to_all | solution.py:21
  30.5 13.2 %all_gather.15 = f32[8,144,144]{2,1,0:T(8,128)S(1)} all-gather(f32[1,144,144]{2,1,0:T(8,128)} %all_gather_reshape.3), channel_id=1, replica_groups=mesh['area'=4,'dev'=8] {'dev'}, dimensions={0}, use_global_device_ids=true | all-gather | bytes 746496 | tf_op jit(solution)/shard_map/all_gather | solution.py:10
  44.9 11.7 %cholesky.50 = f32[128,128]{1,0:T(8,128)S(1)} custom-call(f32[128,128]{1,0:T(8,128)S(1)} %cholesky.121), custom_call_target="Cholesky" | custom-call | tf_op jit(solution)/shard_map/jit(cholesky)/cholesky | solution.py:58
  56.7 9.8 %custom-call.17 = f32[1,128,128]{1,2,0:T(8,128)S(1)} custom-call(f32[1,128,128]{2,1,0:T(8,128)S(1)} %get-tuple-element.103), custom_call_target="InvertDiagBlocksLowerTriangular" | custom-call | tf_op jit(solution)/shard_map/jit(cholesky)/cholesky | solution.py:58
  71.2 19.7 %custom-call.25 = f32[2,128,128]{1,2,0:T(8,128)S(1)} custom-call(f32[2,128,128]{2,1,0:T(8,128)S(1)} %pad_maximum_fusion.9), custom_call_target="InvertDiagBlocksLowerTriangular" | custom-call | tf_op jit(solution)/shard_map/triangular_solve/custom-call.4 | solution.py:17
  95.2 33.1 %reduce-scatter.13.cloned.1.call-done = f32[16,144]{1,0:T(8,128)} async-done(((f32[128,144]{1,0:T(8,128)}), f32[16,144]{1,0:T(8,128)}) %reduce-scatter.13.cloned.1.call-update) | async-done | bytes 9232
  130.9 9.4 %all_gather.16 = f32[144,128]{0,1:T(8,128)S(1)} all-gather(f32[144,16]{0,1:T(8,128)S(1)} %pad_maximum_fusion.10), channel_id=1, replica_groups=mesh['area'=4,'dev'=8] {'dev'}, dimensions={1}, use_global_device_ids=true | all-gather | bytes 82944 | tf_op jit(solution)/shard_map/all_gather | solution.py:88
  142.5 4.6 all-to-all-start.1
  151.6 5.0 %fusion.5 = f32[3,512,128]{2,0,1:T(4,128)S(1)} fusion(f32[3,511,128]{2,0,1:T(4,128)} %copy.233, f32[3,1,128]{2,0,1:T(4,128)S(1)} %copy.234, f32[3,512]{0,1:T(8,128)S(1)} %copy.116, f32[3,512]{0,1:T(8,128)S(1)} %copy.113, f32[3,512,128]{2,1,0:T(8,128)S(1)} %copy-done.2), kind=kLoop, calls=%fused_computation.61 | loop fusion | flops 786432 | bytes 2371584 | tf_op jit(solution)/shard_map/add | solution.py:104
  156.6 4.5 fusion.4
  173.3 18.9 %all_to_all.84 = f32[32,8,384]{2,1,0:T(8,128)} all-to-all(f32[32,8,384]{2,1,0:T(8,128)S(1)} %bitcast.341), channel_id=1, replica_groups=mesh['area'=4,'dev'=8] {'area','dev'}, dimensions={0} | all-to-all | bytes 786432 | tf_op jit(solution)/shard_map/all_to_all | solution.py:21
  196.9 31.6 %reduce-scatter.15.cloned.1.call-done = f32[16,144]{1,0:T(8,128)} async-done(((f32[128,144]{1,0:T(8,128)}), f32[16,144]{1,0:T(8,128)}) %reduce-scatter.15.cloned.1.call-update) | async-done | bytes 9232
  232.4 9.6 %all_gather.17 = f32[144,128]{0,1:T(8,128)S(1)} all-gather(f32[144,16]{0,1:T(8,128)S(1)} %pad_maximum_fusion.11), channel_id=1, replica_groups=mesh['area'=4,'dev'=8] {'dev'}, dimensions={1}, use_global_device_ids=true | all-gather | bytes 82944 | tf_op jit(solution)/shard_map/all_gather | solution.py:88
  244.8 4.7 %all-to-all-start.3 = ((f32[32,8,384]{2,1,0:T(8,128)}), f32[32,8,384]{2,1,0:T(8,128)}, u32[]{:S(2)}, u32[]{:S(2)}) async-start(f32[32,8,384]{2,1,0:T(8,128)} %fusion.55), calls=%async_computation.3 | async-start | bytes 786432 | tf_op jit(solution)/shard_map/all_to_all | solution.py:25
  255.6 7.1 %all-to-all-done.3 = f32[32,8,384]{2,1,0:T(8,128)} async-done(((f32[32,8,384]{2,1,0:T(8,128)}), f32[32,8,384]{2,1,0:T(8,128)}, u32[]{:S(2)}, u32[]{:S(2)}) %all-to-all-start.3) | async-done | bytes 393248 | tf_op jit(solution)/shard_map/all_to_all | solution.py:25
  274.9 15.6 %all_to_all.85 = f32[32,8,384]{2,1,0:T(8,128)S(1)} all-to-all(f32[32,8,384]{2,1,0:T(8,128)S(1)} %bitcast.344), channel_id=1, replica_groups=mesh['area'=4,'dev'=8] {'area','dev'}, dimensions={0} | all-to-all | bytes 786432 | tf_op jit(solution)/shard_map/all_to_all | solution.py:21
  293.6 31.5 %reduce-scatter.17.cloned.1.call-done = f32[16,144]{1,0:T(8,128)} async-done(((f32[128,144]{1,0:T(8,128)}), f32[16,144]{1,0:T(8,128)}) %reduce-scatter.17.cloned.1.call-update) | async-done | bytes 9232
  329.1 9.2 %all_gather.18 = f32[144,128]{0,1:T(8,128)S(1)} all-gather(f32[144,16]{0,1:T(8,128)S(1)} %pad_maximum_fusion.12), channel_id=1, replica_groups=mesh['area'=4,'dev'=8] {'dev'}, dimensions={1}, use_global_device_ids=true | all-gather | bytes 82944 | tf_op jit(solution)/shard_map/all_gather | solution.py:88
  340.5 4.7 %all-to-all-start.5 = ((f32[32,8,384]{2,1,0:T(8,128)}), f32[32,8,384]{2,1,0:T(8,128)}, u32[]{:S(2)}, u32[]{:S(2)}) async-start(f32[32,8,384]{2,1,0:T(8,128)} %fusion.53), calls=%async_computation.5 | async-start | bytes 786432 | tf_op jit(solution)/shard_map/all_to_all | solution.py:25
  351.5 6.9 %all-to-all-done.5 = f32[32,8,384]{2,1,0:T(8,128)} async-done(((f32[32,8,384]{2,1,0:T(8,128)}), f32[32,8,384]{2,1,0:T(8,128)}, u32[]{:S(2)}, u32[]{:S(2)}) %all-to-all-start.5) | async-done | bytes 393248 | tf_op jit(solution)/shard_map/all_to_all | solution.py:25
  370.5 15.6 %all_to_all.86 = f32[32,8,384]{2,1,0:T(8,128)S(1)} all-to-all(f32[32,8,384]{2,1,0:T(8,128)S(1)} %bitcast.339), channel_id=1, replica_groups=mesh['area'=4,'dev'=8] {'area','dev'}, dimensions={0} | all-to-all | bytes 786432 | tf_op jit(solution)/shard_map/all_to_all | solution.py:21
  392.8 28.1 %reduce-scatter.19.cloned.1.call-done = f32[16,144]{1,0:T(8,128)} async-done(((f32[128,144]{1,0:T(8,128)}), f32[16,144]{1,0:T(8,128)}) %reduce-scatter.19.cloned.1.call-update) | async-done | bytes 9232
  424.7 9.2 %all_gather.19 = f32[144,128]{0,1:T(8,128)S(1)} all-gather(f32[144,16]{0,1:T(8,128)S(1)} %pad_maximum_fusion.13), channel_id=1, replica_groups=mesh['area'=4,'dev'=8] {'dev'}, dimensions={1}, use_global_device_ids=true | all-gather | bytes 82944 | tf_op jit(solution)/shard_map/all_gather | solution.py:88
  436.8 4.8 %all-to-all-start.7 = ((f32[32,8,384]{2,1,0:T(8,128)}), f32[32,8,384]{2,1,0:T(8,128)S(1)}, u32[]{:S(2)}, u32[]{:S(2)}) async-start(f32[32,8,384]{2,1,0:T(8,128)} %fusion.51), calls=%async_computation.7 | async-start | bytes 786432 | tf_op jit(solution)/shard_map/all_to_all | solution.py:25
  (353 shorter events, 136.9 us)
Async XLA Ops:
  16.4 74.5 %all-to-all-start = ((f32[32,8,384]{2,1,0:T(8,128)}), f32[32,8,384]{2,1,0:T(8,128)}, u32[]{:S(2)}, u32[]{:S(2)}) async-start(f32[32,8,384]{2,1,0:T(8,128)} %bitcast.11), calls=%async_computation | async-start | bytes 786432 | tf_op jit(solution)/shard_map/all_to_all | solution.py:21
  23.9 104.5 %reduce-scatter.13.cloned.1.call-start = ((), (), s32[]{:S(2)}) async-start(), calls=%async_computation.12 | async-start | bytes 147456
  30.5 61.6 %copy-start.41 = (s32[1,256]{1,0:T(1,128)S(1)}, s32[1,256]{1,0:T(1,128)}, u32[]{:S(2)}) copy-start(s32[1,256]{1,0:T(1,128)} %param.23) | copy-start | bytes 3076
  30.5 62.8 %copy-start.1 = (f32[3,3,64]{1,0,2:T(4,128)S(1)}, f32[3,3,64]{1,0,2:T(4,128)}, u32[]{:S(2)}) copy-start(f32[3,3,64]{1,0,2:T(4,128)} %copy.101) | copy-start | bytes 6916
  30.5 63.4 %copy-start.43 = (s32[48]{0:T(128)S(1)}, s32[48]{0:T(128)}, u32[]{:S(2)}) copy-start(s32[48]{0:T(128)} %copy-done.42) | copy-start | bytes 580
  30.5 63.5 %copy-start.46 = (s32[48]{0:T(128)S(1)}, s32[48]{0:T(128)}, u32[]{:S(2)}) copy-start(s32[48]{0:T(128)} %copy-done.45) | copy-start | bytes 580
  30.5 63.5 %copy-start.49 = (s32[64]{0:T(128)S(1)}, s32[64]{0:T(128)}, u32[]{:S(2)}) copy-start(s32[64]{0:T(128)} %copy-done.48) | copy-start | bytes 772
  30.5 64.6 %slice-start = ((f32[3,512]{1,0:T(4,128)}), f32[3,1]{1,0:T(4,128)S(1)}, s32[]{:S(2)}) async-start(f32[3,512]{1,0:T(4,128)} %param.18), calls=%async_computation.16 | async-start | bytes 4096 | tf_op jit(solution)/shard_map/jit(_roll_static)/slice | solution.py:62
  56.6 90.6 %copy-start.68 = (s32[128]{0:T(128)S(1)}, s32[128]{0:T(128)}, u32[]{:S(2)}) copy-start(s32[128]{0:T(128)} %copy-done.67) | copy-start | bytes 1540
  56.6 91.2 %copy-start.3 = (f32[3,512,128]{2,1,0:T(8,128)S(1)}, f32[3,512,128]{2,1,0:T(8,128)}, u32[]{:S(2)}) copy-start(f32[3,512,128]{2,1,0:T(8,128)} %param.16) | copy-start | bytes 2359300
  66.7 81.2 %copy-start.2 = (f32[3,512,128]{2,1,0:T(8,128)S(1)}, f32[3,512,128]{2,1,0:T(8,128)}, u32[]{:S(2)}) copy-start(f32[3,512,128]{2,1,0:T(8,128)} %param.17) | copy-start | bytes 2359300
  71.0 76.9 %copy-start.29 = (f32[144,144]{1,0:T(8,128)}, f32[144,144]{1,0:T(8,128)S(1)}, u32[]{:S(2)}) copy-start(f32[144,144]{1,0:T(8,128)S(1)} %select_select_fusion) | copy-start | bytes 248836
  90.9 57.2 %copy-start.16 = (f32[2,128,128]{1,2,0:T(8,128)}, f32[2,128,128]{1,2,0:T(8,128)S(1)}, u32[]{:S(2)}) copy-start(f32[2,128,128]{1,2,0:T(8,128)S(1)} %custom-call.25) | copy-start | bytes 393220
  142.5 18.6 %all-to-all-start.1 = ((f32[32,8,384]{2,1,0:T(8,128)}), f32[32,8,384]{2,1,0:T(8,128)S(1)}, u32[]{:S(2)}, u32[]{:S(2)}) async-start(f32[32,8,384]{2,1,0:T(8,128)} %fusion.57), calls=%async_computation.1 | async-start | bytes 786432 | tf_op jit(solution)/shard_map/all_to_all | solution.py:25
  147.1 81.4 %reduce-scatter.15.cloned.1.call-start = ((), (), s32[]{:S(2)}) async-start(), calls=%async_computation.13 | async-start | bytes 147456
  151.6 98.2 %copy-start.10 = (f32[3,512]{0,1:T(8,128)}, f32[3,512]{0,1:T(8,128)S(1)}, u32[]{:S(2)}) copy-start(f32[3,512]{0,1:T(8,128)S(1)} %copy.108) | copy-start | bytes 18436
  162.2 67.0 %copy-start.17 = (f32[2,128,128]{1,2,0:T(8,128)S(1)}, f32[2,128,128]{1,2,0:T(8,128)}, u32[]{:S(2)}) copy-start(f32[2,128,128]{1,2,0:T(8,128)} %copy-done.16) | copy-start | bytes 393220
  244.8 17.9 %all-to-all-start.3 = ((f32[32,8,384]{2,1,0:T(8,128)}), f32[32,8,384]{2,1,0:T(8,128)}, u32[]{:S(2)}, u32[]{:S(2)}) async-start(f32[32,8,384]{2,1,0:T(8,128)} %fusion.55), calls=%async_computation.3 | async-start | bytes 786432 | tf_op jit(solution)/shard_map/all_to_all | solution.py:25
  249.5 75.6 %reduce-scatter.17.cloned.1.call-start = ((), (), s32[]{:S(2)}) async-start(), calls=%async_computation.14 | async-start | bytes 147456
  264.8 61.1 %copy-start.18 = (f32[2,128,128]{1,2,0:T(8,128)S(1)}, f32[2,128,128]{1,2,0:T(8,128)}, u32[]{:S(2)}) copy-start(f32[2,128,128]{1,2,0:T(8,128)} %copy-done.16) | copy-start | bytes 393220
  340.5 17.9 %all-to-all-start.5 = ((f32[32,8,384]{2,1,0:T(8,128)}), f32[32,8,384]{2,1,0:T(8,128)}, u32[]{:S(2)}, u32[]{:S(2)}) async-start(f32[32,8,384]{2,1,0:T(8,128)} %fusion.53), calls=%async_computation.5 | async-start | bytes 786432 | tf_op jit(solution)/shard_map/all_to_all | solution.py:25
  345.2 75.6 %reduce-scatter.19.cloned.1.call-start = ((), (), s32[]{:S(2)}) async-start(), calls=%async_computation.15 | async-start | bytes 147456
  392.8 52.9 %copy-start.9 = (f32[3,512]{0,1:T(8,128)S(1)}, f32[3,512]{0,1:T(8,128)}, u32[]{:S(2)}) copy-start(f32[3,512]{0,1:T(8,128)} %copy-done.6) | copy-start | bytes 18436
  436.8 18.0 %all-to-all-start.7 = ((f32[32,8,384]{2,1,0:T(8,128)}), f32[32,8,384]{2,1,0:T(8,128)S(1)}, u32[]{:S(2)}, u32[]{:S(2)}) async-start(f32[32,8,384]{2,1,0:T(8,128)} %fusion.51), calls=%async_computation.7 | async-start | bytes 786432 | tf_op jit(solution)/shard_map/all_to_all | solution.py:25
  (55 other events, 615.6 us)
Sparse Core Ops, SparseCore 0:
  95.3 33.0 reduce-scatter.12
  197.1 31.3 reduce-scatter.14
  293.8 31.3 reduce-scatter.16
  389.4 31.3 reduce-scatter.18
